TPU v7x, 32 devices: a whole 2x2x4 slice. The times are simulated.
32 devices in a mesh: groups: 2 (over y), latent: 4 (over z), dp: 2 (over x), sub: 2 (over core).
Axes of the slice: x: 2, y: 2, z: 4, core: 2. Of those that a mesh axis runs over, the one named last changes fastest.
Arguments:
- inputs: bfloat16 [448, 4096], P(('groups', 'latent'), ('dp', 'sub')), parts along dimension 0, may hold values from -6 to 6
- dec_bias: float32 [8192], P(('groups', 'dp', 'sub')), parts along dimension 0, may hold values from -3 to 3
- enc_master: float32 [1664, 4096], P(('groups', 'latent'), ('dp', 'sub')), parts along dimension 0, may hold values from -0.09375 to 0.09375
- enc_bias: float32 [1664], P(('groups', 'latent')), parts along dimension 0, may hold values from -3 to 3
- dec_master: float32 [1664, 4096], P(('groups', 'latent'), ('dp', 'sub')), parts along dimension 0, may hold values from -0.25 to 0.25
- enc_m: float32 [1664, 4096], P(('groups', 'latent'), ('dp', 'sub')), parts along dimension 0, may hold values from -0.0006 to 0.0006
- enc_v: float32 [1664, 4096], P(('groups', 'latent'), ('dp', 'sub')), parts along dimension 0, may hold values from 1e-09 to 1e-07
- dec_m: float32 [1664, 4096], P(('groups', 'latent'), ('dp', 'sub')), parts along dimension 0, may hold values from -0.0006 to 0.0006
- dec_v: float32 [1664, 4096], P(('groups', 'latent'), ('dp', 'sub')), parts along dimension 0, may hold values from 1e-09 to 1e-07
- bias_m: float32 [1664], P(('groups', 'latent')), parts along dimension 0, may hold values from -0.0006 to 0.0006
- bias_v: float32 [1664], P(('groups', 'latent')), parts along dimension 0, may hold values from 1e-09 to 1e-07
Outputs:
- enc_new: float32 [1664, 4096], P(('groups', 'latent'), ('dp', 'sub')), parts along dimension 0
- bias_new: float32 [1664], P(('groups', 'latent')), parts along dimension 0
- dec_new: float32 [1664, 4096], P(('groups', 'latent'), ('dp', 'sub')), parts along dimension 0
- enc_m_new: float32 [1664, 4096], P(('groups', 'latent'), ('dp', 'sub')), parts along dimension 0
- enc_v_new: float32 [1664, 4096], P(('groups', 'latent'), ('dp', 'sub')), parts along dimension 0
- dec_m_new: float32 [1664, 4096], P(('groups', 'latent'), ('dp', 'sub')), parts along dimension 0
- dec_v_new: float32 [1664, 4096], P(('groups', 'latent'), ('dp', 'sub')), parts along dimension 0
- bias_m_new: float32 [1664], P(('groups', 'latent')), parts along dimension 0
- bias_v_new: float32 [1664], P(('groups', 'latent')), parts along dimension 0
- loss: float32 [2], P('groups'), parts along dimension 0
There are 2 independent parts, one for each index of `groups`. A program takes and returns all parts, laid end to end along the dimension named above; each array names one. Nothing has to cross between parts.
All inputs are finite; a program needn't handle non-finite values.
Results may differ from a plain program's by a relative error of at most 0.0049.
Values may be sent and summed in bfloat16 or wider, within the bound.
A program may use at most 64 MiB of HBM per device.

v0:
```python
import jax
import jax.numpy as jnp
from jax import lax
from jax.sharding import PartitionSpec as P

sparsity_coef = 5.0
clip_norm = 1.0
learn_rate = 0.01
beta_one = 0.9
beta_two = 0.999
adam_step = 100


def adam_update(master, moment_one, moment_two, gradient):
    new_one = beta_one * moment_one + (1.0 - beta_one) * gradient
    new_two = beta_two * moment_two + (1.0 - beta_two) * gradient * gradient
    fix_one = 1.0 - beta_one**adam_step
    fix_two = 1.0 - beta_two**adam_step
    updated = master - learn_rate * (new_one / fix_one) / (jnp.sqrt(new_two / fix_two) + 1e-08)
    return (updated, new_one, new_two)


def per_device(
    inputs, dec_bias, enc_master, enc_bias, dec_master, enc_m, enc_v, dec_m, dec_v, bias_m, bias_v
):
    gathered = lax.all_gather(inputs, "latent", axis=0, tiled=True)
    tokens = gathered.shape[0]
    own_flag = (lax.axis_index(("dp", "sub")) == 0).astype(jnp.float32)
    centered = (gathered.astype(jnp.float32) - dec_bias).astype(jnp.bfloat16)
    enc_copy = enc_master.astype(jnp.bfloat16)
    dec_copy = dec_master.astype(jnp.bfloat16)
    contract = (((1,), (1,)), ((), ()))
    first_dims = (((0,), (0,)), ((), ()))
    pre_part = lax.dot_general(centered, enc_copy, contract, preferred_element_type=jnp.float32)
    norm_part = jnp.sum(dec_master * dec_master, axis=1)
    pre_total, norm_total = lax.psum((pre_part, norm_part), ("dp", "sub"))
    preact = pre_total + enc_bias
    dec_norms = jnp.sqrt(norm_total + 1e-06)
    active = jnp.maximum(preact, 0.0)
    active_b = active.astype(jnp.bfloat16)
    partial_value = jnp.dot(active_b, dec_copy, preferred_element_type=jnp.float32)
    sparse_part = own_flag * jnp.sum(active * dec_norms)
    recon_rows = lax.psum_scatter(partial_value, "latent", scatter_dimension=0, tiled=True)
    residual = recon_rows + dec_bias - inputs.astype(jnp.float32)
    error_part = jnp.sum(residual * residual)
    grad_rows = (residual * (2.0 / tokens)).astype(jnp.bfloat16)
    out_grad = lax.all_gather(grad_rows, "latent", axis=0, tiled=True)
    error_total, sparse_total = lax.psum((error_part, sparse_part), ("latent", "dp", "sub"))
    dec_grad = lax.dot_general(active_b, out_grad, first_dims, preferred_element_type=jnp.float32)
    dec_grad = (
        dec_grad
        + sparsity_coef
        / tokens
        * jnp.sum(active, axis=0)[:, None]
        * dec_master
        / dec_norms[:, None]
    )
    back_part = lax.dot_general(out_grad, dec_copy, contract, preferred_element_type=jnp.float32)
    back = lax.psum(back_part, ("dp", "sub")) + sparsity_coef / tokens * dec_norms
    pre_grad = jnp.where(preact > 0.0, back, 0.0)
    pre_grad_b = pre_grad.astype(jnp.bfloat16)
    enc_grad = lax.dot_general(pre_grad_b, centered, first_dims, preferred_element_type=jnp.float32)
    bias_grad = jnp.sum(pre_grad, axis=0)
    square_part = (
        jnp.sum(enc_grad * enc_grad)
        + jnp.sum(dec_grad * dec_grad)
        + own_flag * jnp.sum(bias_grad * bias_grad)
    )
    grad_square = lax.psum(square_part, ("latent", "dp", "sub"))
    loss = (error_total + sparsity_coef * sparse_total) / tokens
    clip_scale = jnp.minimum(1.0, clip_norm / jnp.sqrt(grad_square + 1e-12))
    enc_new, enc_m_new, enc_v_new = adam_update(enc_master, enc_m, enc_v, clip_scale * enc_grad)
    bias_new, bias_m_new, bias_v_new = adam_update(enc_bias, bias_m, bias_v, clip_scale * bias_grad)
    dec_new, dec_m_new, dec_v_new = adam_update(dec_master, dec_m, dec_v, clip_scale * dec_grad)
    return (
        enc_new,
        bias_new,
        dec_new,
        enc_m_new,
        enc_v_new,
        dec_m_new,
        dec_v_new,
        bias_m_new,
        bias_v_new,
        jnp.reshape(loss, (1,)),
    )


def solution(mesh):
    placed = (
        P(("groups", "latent"), ("dp", "sub")),
        P(("groups", "dp", "sub")),
        P(("groups", "latent"), ("dp", "sub")),
        P(("groups", "latent")),
        P(("groups", "latent"), ("dp", "sub")),
        P(("groups", "latent"), ("dp", "sub")),
        P(("groups", "latent"), ("dp", "sub")),
        P(("groups", "latent"), ("dp", "sub")),
        P(("groups", "latent"), ("dp", "sub")),
        P(("groups", "latent")),
        P(("groups", "latent")),
    )
    return jax.shard_map(
        per_device,
        mesh=mesh,
        in_specs=placed,
        out_specs=(
            P(("groups", "latent"), ("dp", "sub")),
            P(("groups", "latent")),
            P(("groups", "latent"), ("dp", "sub")),
            P(("groups", "latent"), ("dp", "sub")),
            P(("groups", "latent"), ("dp", "sub")),
            P(("groups", "latent"), ("dp", "sub")),
            P(("groups", "latent"), ("dp", "sub")),
            P(("groups", "latent")),
            P(("groups", "latent")),
            P("groups"),
        ),
        check_vma=False,
    )
```

profile of v0, /device:TPU:0, one launch (start us, length us, event | category | flops | bytes accessed | tf_op | source)
XLA Modules:
  0.0 192.7 jit_solution(293579001393840260)
XLA Ops:
  7.2 0.0 copy-start.7
  7.2 0.0 all-reduce.4.cloned.1.call-start
  7.2 17.0 %all_gather.6 = bf16[224,1024]{1,0:T(8,128)(2,1)S(1)} all-gather(bf16[56,1024]{1,0:T(8,128)(2,1)} %param.11), channel_id=1, replica_groups=mesh['groups'=2,'latent'=4,'dp'=2,'sub'=2] {'latent'}, dimensions={0}, use_global_device_ids=true | all-gather | bytes 573440 | tf_op jit(solution)/shard_map/all_gather | solution.py:26
  24.2 2.2 %fusion.2 = f32[224,208]{0,1:T(8,128)} fusion(f32[208,1024]{1,0:T(8,128)} %param.13, bf16[224,1024]{1,0:T(8,128)(2,1)S(1)} %all_gather.6, f32[1024]{0:T(1024)S(1)} %copy-done.7), kind=kOutput, calls=%fused_computation.13 | convolution fusion | flops 96321536 | bytes 1501184 | tf_op jit(solution)/shard_map/dot_general | solution.py:34
  26.5 0.0 all-reduce.4.cloned.1.call-update
  26.5 0.0 reduce-scatter.2.cloned.1.call-start
  26.6 33.0 %all-reduce.4.cloned.1.call-done = f32[224,208]{0,1:T(8,128)} async-done(((f32[224,208]{0,1:T(8,128)}), f32[224,208]{0,1:T(8,128)}) %all-reduce.4.cloned.1.call-update) | async-done | bytes 186384 | tf_op jit(solution)/shard_map/psum | solution.py:36
  59.5 0.0 copy-done
  59.5 2.2 %fusion.7 = f32[224,1024]{1,0:T(8,128)} fusion(f32[208,1024]{1,0:T(8,128)S(1)} %copy-done, f32[224,208]{0,1:T(8,128)} %all-reduce.4.cloned.1.call-done, f32[208]{0:T(256)S(1)} %copy-done.8), kind=kOutput, calls=%fused_computation.23 | convolution fusion | flops 95773184 | bytes 1956672 | tf_op jit(solution)/shard_map/dot_general | solution.py:41
  61.8 0.0 reduce-scatter.2.cloned.1.call-update
  61.8 0.0 copy-start.6
  61.8 0.0 all-reduce.6.cloned.1.call-start
  61.8 0.1 multiply_reduce_fusion.2
  62.0 5.7 %psum.44 = f32[208]{0:T(256)S(1)} all-reduce(f32[208]{0:T(256)S(1)} %multiply_reduce_fusion.2), channel_id=1, replica_groups=mesh['groups'=2,'latent'=4,'dp'=2,'sub'=2] {'dp','sub'}, use_global_device_ids=true, to_apply=%region_4.0 | all-reduce | flops 208 | bytes 1664 | tf_op jit(solution)/shard_map/psum | solution.py:36
  67.6 20.1 %reduce-scatter.2.cloned.1.call-done = f32[56,1024]{1,0:T(8,128)} async-done(((f32[224,1024]{1,0:T(8,128)}), f32[56,1024]{1,0:T(8,128)}) %reduce-scatter.2.cloned.1.call-update) | async-done | bytes 229392 | tf_op jit(solution)/shard_map/reduce_scatter | solution.py:43
  87.8 1.6 multiply_reduce_fusion.3
  89.4 15.4 %all_gather.7 = bf16[224,1024]{1,0:T(8,128)(2,1)S(1)} all-gather(bf16[56,1024]{1,0:T(8,128)(2,1)S(1)} %get-tuple-element.26), channel_id=1, replica_groups=mesh['groups'=2,'latent'=4,'dp'=2,'sub'=2] {'latent'}, dimensions={0}, use_global_device_ids=true | all-gather | bytes 573440 | tf_op jit(solution)/shard_map/all_gather | solution.py:47
  104.8 1.0 fusion.5
  105.8 0.0 all-reduce.6.cloned.1.call-update
  105.9 29.6 %all-reduce.6.cloned.1.call-done = f32[224,208]{0,1:T(8,128)} async-done(((f32[224,208]{0,1:T(8,128)}), f32[224,208]{0,1:T(8,128)}) %all-reduce.6.cloned.1.call-update) | async-done | bytes 186384 | tf_op jit(solution)/shard_map/psum | solution.py:59
  135.5 1.9 multiply_reduce_fusion.4
  137.4 0.6 multiply_reduce_fusion.5
  139.3 1.0 multiply_reduce_fusion.1
  140.3 1.8 multiply_reduce_fusion
  143.5 32.7 %all-reduce = (f32[]{:T(128)}, f32[]{:T(128)}, f32[]{:T(128)}) all-reduce(f32[]{:T(128)S(6)} %add.103, f32[]{:T(128)} %get-tuple-element.25, f32[]{:T(128)S(6)} %mul.193), channel_id=1, replica_groups=mesh['groups'=2,'latent'=4,'dp'=2,'sub'=2] {'latent','dp','sub'}, use_global_device_ids=true, to_apply=%region_10.11 | all-reduce | flops 3 | bytes 24 | tf_op jit(solution)/shard_map/psum | solution.py:69
  178.2 0.0 copy-start.9
  178.2 0.0 copy-done.10
  178.2 0.7 copy-done.9
  178.9 0.6 divide_subtract_fusion.2
  179.4 3.7 %divide_subtract_fusion = (f32[208,1024]{1,0:T(8,128)}, f32[208,1024]{1,0:T(8,128)}, f32[208,1024]{1,0:T(8,128)}) fusion(f32[208,1024]{1,0:T(8,128)S(1)} %copy-done, f32[208,1024]{1,0:T(8,128)} %get-tuple-element.32, f32[]{:T(128)S(6)} %min.3, f32[208,1024]{1,0:T(8,128)} %param.18, f32[208,1024]{1,0:T(8,128)} %param.19), kind=kLoop, calls=%fused_computation.6 | loop fusion | flops 2768896 | bytes 5963780 | tf_op jit(solution)/shard_map/sub | solution.py:19
  183.2 0.0 copy-done.3
  183.2 1.9 divide_subtract_fusion.1
  (16 shorter events, 0.0 us)
Async XLA Ops:
  7.2 17.1 %copy-start.7 = (f32[1024]{0:T(1024)S(1)}, f32[1024]{0:T(1024)}, u32[]{:S(2)}) copy-start(f32[1024]{0:T(1024)} %param.12) | copy-start | bytes 12292
  7.2 52.3 %all-reduce.4.cloned.1.call-start = ((), (), s32[]{:S(2)}) async-start(), calls=%async_computation.1 | async-start | bytes 425984 | tf_op jit(solution)/shard_map/psum | solution.py:36
  24.2 35.3 %copy-start = (f32[208,1024]{1,0:T(8,128)S(1)}, f32[208,1024]{1,0:T(8,128)}, u32[]{:S(2)}) copy-start(f32[208,1024]{1,0:T(8,128)} %param.15) | copy-start | bytes 2555908
  26.5 33.0 %copy-start.8 = (f32[208]{0:T(256)S(1)}, f32[208]{0:T(256)}, u32[]{:S(2)}) copy-start(f32[208]{0:T(256)} %param.14) | copy-start | bytes 2500
  26.5 61.3 %reduce-scatter.2.cloned.1.call-start = ((), (), s32[]{:S(2)}) async-start(), calls=%async_computation.2 | async-start | bytes 1146880 | tf_op jit(solution)/shard_map/reduce_scatter | solution.py:43
  61.8 26.0 %copy-start.6 = (bf16[56,1024]{1,0:T(8,128)(2,1)S(1)}, bf16[56,1024]{1,0:T(8,128)(2,1)}, u32[]{:S(2)}) copy-start(bf16[56,1024]{1,0:T(8,128)(2,1)} %param.11) | copy-start | bytes 344068
  61.8 73.7 %all-reduce.6.cloned.1.call-start = ((), (), s32[]{:S(2)}) async-start(), calls=%async_computation.3 | async-start | bytes 425984 | tf_op jit(solution)/shard_map/psum | solution.py:59
  105.8 29.7 %copy-start.2 = (f32[224,208]{0,1:T(8,128)S(1)}, f32[224,208]{0,1:T(8,128)}, u32[]{:S(2)}) copy-start(f32[224,208]{0,1:T(8,128)} %all-reduce.4.cloned.1.call-done) | copy-start | bytes 559108
  135.5 3.8 %copy-start.5 = (f32[224,208]{0,1:T(8,128)S(1)}, f32[224,208]{0,1:T(8,128)}, u32[]{:S(2)}) copy-start(f32[224,208]{0,1:T(8,128)} %all-reduce.6.cloned.1.call-done) | copy-start | bytes 559108
  140.3 37.9 %copy-start.10 = (f32[208]{0:T(256)S(1)}, f32[208]{0:T(256)}, u32[]{:S(2)}) copy-start(f32[208]{0:T(256)} %param.21) | copy-start | bytes 2500
  178.2 0.7 copy-start.9
  179.4 3.7 %copy-start.1 = (f32[208,1024]{1,0:T(8,128)S(1)}, f32[208,1024]{1,0:T(8,128)}, u32[]{:S(2)}) copy-start(f32[208,1024]{1,0:T(8,128)} %param.13) | copy-start | bytes 2555908
  179.4 3.7 %copy-start.3 = (f32[208,1024]{1,0:T(8,128)S(1)}, f32[208,1024]{1,0:T(8,128)}, u32[]{:S(2)}) copy-start(f32[208,1024]{1,0:T(8,128)} %param.16) | copy-start | bytes 2555908
  179.4 3.7 %copy-start.4 = (f32[208,1024]{1,0:T(8,128)S(1)}, f32[208,1024]{1,0:T(8,128)}, u32[]{:S(2)}) copy-start(f32[208,1024]{1,0:T(8,128)} %param.17) | copy-start | bytes 2555908
Sparse Core Ops, SparseCore 0:
  26.6 32.8 all-reduce.3
  61.9 25.7 reduce-scatter.1
  106.0 29.5 all-reduce.5
where the time goes:
time: 193 us
  waiting for transfers between devices  82.8 us (43%)
  blocking collectives  70.8 us (37%)
  between operations  19.5 us (10%)
  other arithmetic  10.4 us (5%)
  matrix products  8.34 us (4%)
    psum x1, waiting for transfers between devices, per_device(): pre_total, norm_total = lax.psum((pre_part, norm_part), ('dp', 'sub'))  33 us
    psum x1, blocking collectives, per_device(): grad_square = lax.psum(square_part, ('latent', 'dp', 'sub'))  32.7 us
    psum x1, waiting for transfers between devices, per_device(): lax.psum(back_part, ('dp', 'sub')) + sparsity_coef / tokens * dec_norms  29.6 us
    reduce_scatter x1, waiting for transfers between devices, per_device(): lax.psum_scatter(partial_value, 'latent', scatter_dimension=0, tiled=True)  20.1 us
    all_gather x1, blocking collectives, per_device(): gathered = lax.all_gather(inputs, 'latent', axis=0, tiled=True)  17 us
    all_gather x1, blocking collectives, per_device(): out_grad = lax.all_gather(grad_rows, 'latent', axis=0, tiled=True)  15.4 us
    sub x3, other arithmetic, adam_update(): master - learn_rate * (new_one / fix_one) / (jnp.sqrt(new_two / fix_two)...  6.16 us
    psum x1, blocking collectives, per_device(): pre_total, norm_total = lax.psum((pre_part, norm_part), ('dp', 'sub'))  5.66 us
  transfers between devices with their start and end apart: 3, of which 3 were waited for; matrix products, arithmetic and copies ran while one was open for 0% of the time, Pallas kernels for 0%

commit v1 on v0

v1 whole, which is shorter than its diff:
```python
import functools

import jax
import jax.numpy as jnp
from jax import lax
from jax.experimental import pallas as pl
from jax.experimental.pallas import tpu as pltpu
from jax.sharding import PartitionSpec as P

sparsity_coef = 5.0
clip_norm = 1.0
learn_rate = 0.01
beta_one = 0.9
beta_two = 0.999
adam_step = 100

MESH = pl.DeviceIdType.MESH
F32 = jnp.float32
BF16 = jnp.bfloat16
NT = (((1,), (1,)), ((), ()))
TN = (((0,), (0,)), ((), ()))


def adam_update(master, moment_one, moment_two, gradient):
    new_one = beta_one * moment_one + (1.0 - beta_one) * gradient
    new_two = beta_two * moment_two + (1.0 - beta_two) * gradient * gradient
    fix_one = 1.0 - beta_one**adam_step
    fix_two = 1.0 - beta_two**adam_step
    updated = master - learn_rate * (new_one / fix_one) / (jnp.sqrt(new_two / fix_two) + 1e-08)
    return (updated, new_one, new_two)


def when(cond):
    if isinstance(cond, bool):
        return (lambda f: f()) if cond else (lambda f: None)
    return pl.when(cond)


def steps(low, high, body, unroll):
    if unroll:
        for j in range(low, high):
            body(j)
    else:
        lax.fori_loop(low, high, lambda j, _: (body(j), 0)[1], 0)


def kernel(
    Z, X, C, rows, x_ref, bias_ref, enc_bias_ref, enc_hbm, dec_hbm,
    enc_grad_ref, dec_grad_ref, bias_grad_ref, scalar_ref,
    enc_f, dec_f, enc_b, dec_b,
    cent_tx, cent_rx, cent, part_tx, part_rx, norm_tx, norm_rx, norm_row, act, recon_own,
    recon_tx, recon_rx, grad_tx, grad_rx, grad, back_tx, back_rx, pre, loss_acc, square_acc,
    one_rx, two_tx, two_rx,
    load_sem, cent_s, cent_r, part_s, part_r, norm_s, norm_r, act_s, act_r,
    recon_s, recon_r, grad_s, grad_r, back_s, back_r, pre_s, pre_r, one_s, one_r, two_s, two_r,
):
    n = X * C
    B = Z // n
    unroll = Z <= 4
    pad = cent.shape[1]
    width = cent.shape[2]
    half = width // 2
    lat = enc_f.shape[0]
    tokens = Z * rows
    z = lax.axis_index("latent")
    f = lax.axis_index("dp") * C + lax.axis_index("sub")

    def zdev(k):
        return {"latent": lax.rem(z + k, Z)}

    def fdev(q):
        return {"dp": lax.div(q, C), "sub": lax.rem(q, C)}

    def fpeer(k):
        return lax.rem(f + k, n)

    def remote(src, dst, s, r, dev):
        return pltpu.make_async_remote_copy(
            src_ref=src, dst_ref=dst, send_sem=s, recv_sem=r, device_id=dev, device_id_type=MESH
        )

    load_enc = pltpu.make_async_copy(enc_hbm, enc_f, load_sem.at[0])
    load_dec = pltpu.make_async_copy(dec_hbm, dec_f, load_sem.at[1])
    load_enc.start()
    load_dec.start()

    barrier = pltpu.get_barrier_semaphore()
    for k in range(1, Z):
        pl.semaphore_signal(barrier, inc=1, device_id=zdev(k), device_id_type=MESH)
    for k in range(1, n):
        pl.semaphore_signal(barrier, inc=1, device_id=fdev(fpeer(k)), device_id_type=MESH)

    def pack(ref, value):
        ref[...] = jnp.concatenate([value[:, :half], value[:, half:]], axis=0).astype(BF16)

    def unpack(ref):
        both = ref[...].astype(F32)
        return both[:rows], both[rows:]

    def place(ref, left, right):
        ref[:rows, :half] = left.astype(BF16)
        ref[:rows, half:] = right.astype(BF16)
        ref[rows:, :] = jnp.zeros((pad - rows, width), BF16)

    x_own = x_ref[...].astype(F32)
    centered = x_own - bias_ref[...]
    pack(cent_tx, centered)
    place(cent.at[0], centered[:, :half], centered[:, half:])
    pl.semaphore_wait(barrier, Z - 1 + n - 1)

    def cent_copy(k):
        return remote(cent_tx, cent_rx.at[Z - k], cent_s.at[k], cent_r.at[Z - k], zdev(k))

    def recon_copy(j):
        return remote(recon_tx.at[j], recon_rx.at[Z - j], recon_s.at[j], recon_r.at[Z - j], zdev(j))

    def grad_copy(k):
        return remote(grad_tx, grad_rx.at[Z - k], grad_s.at[k], grad_r.at[Z - k], zdev(k))

    def norm_copy(k):
        return remote(norm_tx, norm_rx.at[f], norm_s.at[k], norm_r.at[f], fdev(fpeer(k)))

    def part_copy(tx, rx, s, r, j):
        return remote(tx.at[j], rx.at[j % B, f], s.at[j], r.at[j % B, f], fdev(j // B))

    def arrival(rx, s, r, jj, k):
        q = fpeer(k)
        return remote(rx.at[jj, q], rx.at[jj, q], s.at[0], r.at[jj, q], fdev(q))

    def share_copy(buf, s, r, j, k):
        return remote(buf.at[j], buf.at[j], s.at[j % B, k], r.at[j], fdev(fpeer(k)))

    def shared(buf, s, r, j):
        return remote(buf.at[j], buf.at[j], s.at[0, 0], r.at[j], fdev(fpeer(1)))

    for k in range(1, Z):
        cent_copy(k).start()

    load_dec.wait()
    dec = dec_f[...]
    dec_b[...] = dec.astype(BF16)
    column = jnp.sum(dec * dec, axis=1, keepdims=True)
    diag = lax.broadcasted_iota(jnp.int32, (lat, lat), 0) == lax.broadcasted_iota(
        jnp.int32, (lat, lat), 1
    )
    row = jnp.sum(jnp.where(diag, column, 0.0), axis=0, keepdims=True)
    norm_tx[...] = jnp.broadcast_to(row, norm_tx.shape)
    norm_rx[f] = jnp.broadcast_to(row, norm_tx.shape)
    for k in range(1, n):
        norm_copy(k).start()
    load_enc.wait()
    enc_b[...] = enc_f[...].astype(BF16)
    loss_acc[...] = jnp.zeros_like(loss_acc)

    def sum_parts(rx, s, r, jj):
        for k in range(1, n):
            arrival(rx, s, r, jj, k).wait_recv()
        total = rx[jj, 0]
        for q in range(1, n):
            total = total + rx[jj, q]
        return total

    def send_part(value, tx, rx, s, r, j):
        owner = j // B

        @pl.when(f == owner)
        def _():
            rx[j % B, f] = value

        @pl.when(f != owner)
        def _():
            tx[j] = value
            part_copy(tx, rx, s, r, j).start()

    def set_shared(buf, s, r, j, value):
        buf[j, :rows, :] = value.astype(BF16)
        buf[j, rows:, :] = jnp.zeros((pad - rows, lat), BF16)
        for k in range(1, n):
            share_copy(buf, s, r, j, k).start()

    def encode(j):
        @when(j > 0)
        def _():
            remote(cent_tx, cent_rx.at[j], cent_s.at[0], cent_r.at[j], zdev(1)).wait_recv()
            place(cent.at[j], *unpack(cent_rx.at[j]))

        value = lax.dot_general(cent[j], enc_b[...], NT, preferred_element_type=F32)[:rows]
        send_part(value, part_tx, part_rx, part_s, part_r, j)

    def activate(j):
        @pl.when(f == j // B)
        def _():
            total = sum_parts(part_rx, part_s, part_r, j % B)
            active = jnp.maximum(total + enc_bias_ref[...], 0.0)
            set_shared(act, act_s, act_r, j, active)
            loss_acc[:, :lat] += sparsity_coef * jnp.sum(
                active * norm_row[...], axis=0, keepdims=True
            )

    def decode(j):
        @pl.when(f != j // B)
        def _():
            shared(act, act_s, act_r, j).wait_recv()

        value = jnp.dot(act[j], dec_b[...], preferred_element_type=F32)[:rows]

        @when(j == 0)
        def _():
            recon_own[...] = value

        @when(j > 0)
        def _():
            pack(recon_tx.at[j], value)
            recon_copy(j).start()

    def finish_norms():
        for k in range(1, n):
            q = fpeer(k)
            remote(norm_tx, norm_rx.at[q], norm_s.at[0], norm_r.at[q], fdev(q)).wait_recv()
        total = norm_rx[0]
        for q in range(1, n):
            total = total + norm_rx[q]
        norm_row[...] = jnp.sqrt(total[:1] + 1e-06)

    if unroll:
        encode(0)
        finish_norms()
        activate(0)
        encode(1)
        for s in range(2, Z + 2):
            if s < Z:
                encode(s)
            if s - 1 < Z:
                activate(s - 1)
            decode(s - 2)
    else:
        finish_norms()
        steps(0, Z, encode, False)
        steps(0, Z, activate, False)
        steps(0, Z, decode, False)

    left = recon_own[:, :half]
    right = recon_own[:, half:]

    def add_rows(j, carry):
        remote(cent_tx, recon_rx.at[j], recon_s.at[0], recon_r.at[j], zdev(1)).wait_recv()
        one, two = unpack(recon_rx.at[j])
        return carry[0] + one, carry[1] + two

    if unroll:
        for j in range(1, Z):
            left, right = add_rows(j, (left, right))
    else:
        left, right = lax.fori_loop(1, Z, add_rows, (left, right))
    residual = jnp.concatenate([left, right], axis=1) + bias_ref[...] - x_own
    out_grad = residual * (2.0 / tokens)
    pack(grad_tx, out_grad)
    for k in range(1, Z):
        grad_copy(k).start()
    place(grad.at[0], out_grad[:, :half], out_grad[:, half:])
    error = jnp.sum(residual * residual, axis=0, keepdims=True)
    loss_acc[...] += error

    def back(j):
        @when(j > 0)
        def _():
            remote(grad_tx, grad_rx.at[j], grad_s.at[0], grad_r.at[j], zdev(1)).wait_recv()
            place(grad.at[j], *unpack(grad_rx.at[j]))

        value = lax.dot_general(grad[j], dec_b[...], NT, preferred_element_type=F32)[:rows]
        send_part(value, back_tx, back_rx, back_s, back_r, j)

    def through(j):
        @pl.when(f == j // B)
        def _():
            total = sum_parts(back_rx, back_s, back_r, j % B)
            total = total + (sparsity_coef / tokens) * norm_row[...]
            value = jnp.where(act[j].astype(F32)[:rows] > 0.0, total, 0.0)
            set_shared(pre, pre_s, pre_r, j, value)

    if unroll:
        back(0)
        for s in range(1, Z + 1):
            if s < Z:
                back(s)
            through(s - 1)
    else:
        steps(0, Z, back, False)
        steps(0, Z, through, False)

    act_all = act[...].reshape(Z * pad, lat)
    act_sum = jnp.sum(act_all.astype(F32), axis=0, keepdims=True)
    coef_row = (sparsity_coef / tokens) * act_sum / norm_row[...]
    coef = jnp.sum(jnp.where(diag, coef_row, 0.0), axis=1, keepdims=True)
    chunk = min(256, width)
    square_acc[...] = jnp.zeros_like(square_acc)
    for c in range(0, width, chunk):
        cols = slice(c, c + chunk)
        g = lax.dot_general(
            act_all, grad[:, :, cols].reshape(Z * pad, chunk), TN, preferred_element_type=F32
        )
        g = g + coef * dec_f[:, cols]
        dec_grad_ref[:, cols] = g
        square_acc[:, :chunk] += jnp.sum(g * g, axis=0, keepdims=True)

    def wait_pre(j):
        @pl.when(f != j // B)
        def _():
            shared(pre, pre_s, pre_r, j).wait_recv()

    steps(0, Z, wait_pre, unroll)
    pre_all = pre[...].reshape(Z * pad, lat)
    bias_grad = jnp.sum(pre_all.astype(F32), axis=0, keepdims=True)
    bias_grad_ref[...] = bias_grad
    for c in range(0, width, chunk):
        cols = slice(c, c + chunk)
        g = lax.dot_general(
            pre_all, cent[:, :, cols].reshape(Z * pad, chunk), TN, preferred_element_type=F32
        )
        enc_grad_ref[:, cols] = g
        square_acc[:, :chunk] += jnp.sum(g * g, axis=0, keepdims=True)

    first = jnp.where(f == 0, 1.0, 0.0)
    square = jnp.sum(square_acc[...], axis=1, keepdims=True) + first * jnp.sum(
        bias_grad * bias_grad, axis=1, keepdims=True
    )
    loss = jnp.sum(loss_acc[...], axis=1, keepdims=True)
    lane = lax.broadcasted_iota(jnp.int32, (8, 128), 1)
    own = jnp.where(lane == 0, loss, jnp.where(lane == 1, square, 0.0))

    one_rx[z] = own

    def one_copy(k):
        return remote(one_rx.at[z], one_rx.at[z], one_s.at[k], one_r.at[z], zdev(k))

    for k in range(1, Z):
        one_copy(k).start()
    for k in range(1, Z):
        src = lax.rem(z + k, Z)
        remote(one_rx.at[src], one_rx.at[src], one_s.at[0], one_r.at[src], zdev(k)).wait_recv()
    total = one_rx[0]
    for k in range(1, Z):
        total = total + one_rx[k]
    two_rx[f] = total

    def two_copy(k):
        return remote(two_rx.at[f], two_rx.at[f], two_s.at[k], two_r.at[f], fdev(fpeer(k)))

    for k in range(1, n):
        two_copy(k).start()
    for k in range(1, n):
        q = fpeer(k)
        remote(two_rx.at[q], two_rx.at[q], two_s.at[0], two_r.at[q], fdev(q)).wait_recv()
    total = two_rx[0]
    for q in range(1, n):
        total = total + two_rx[q]
    scale = jnp.minimum(1.0, clip_norm / jnp.sqrt(total + 1e-12))
    scalar_ref[...] = jnp.where(lane == 0, total * (1.0 / tokens), scale)

    for k in range(1, Z):
        cent_copy(k).wait_send()
        grad_copy(k).wait_send()
        one_copy(k).wait_send()
    for k in range(1, n):
        norm_copy(k).wait_send()
        two_copy(k).wait_send()

    def drain(j):
        @when(j > 0)
        def _():
            recon_copy(j).wait_send()

        @pl.when(f != j // B)
        def _():
            part_copy(part_tx, part_rx, part_s, part_r, j).wait_send()
            part_copy(back_tx, back_rx, back_s, back_r, j).wait_send()

        @pl.when(f == j // B)
        def _():
            for k in range(1, n):
                share_copy(act, act_s, act_r, j, k).wait_send()
                share_copy(pre, pre_s, pre_r, j, k).wait_send()

    steps(0, Z, drain, unroll)


def gradients(Z, X, C, inputs, dec_bias, enc_bias, enc_master, dec_master):
    rows, width = inputs.shape
    lat = enc_master.shape[0]
    n = X * C
    B = Z // n
    pad = -(-rows // 16) * 16
    dma = pltpu.SemaphoreType.DMA
    vm = pltpu.VMEM
    big = jax.ShapeDtypeStruct((lat, width), F32)
    vmem = pl.BlockSpec(memory_space=pltpu.VMEM)
    hbm = pl.BlockSpec(memory_space=pl.ANY)
    packed = (2 * rows, width // 2)
    return pl.pallas_call(
        functools.partial(kernel, Z, X, C, rows),
        out_shape=(
            big,
            big,
            jax.ShapeDtypeStruct((1, lat), F32),
            jax.ShapeDtypeStruct((8, 128), F32),
        ),
        in_specs=[vmem, vmem, vmem, hbm, hbm],
        out_specs=[vmem] * 4,
        scratch_shapes=[
            vm((lat, width), F32),
            vm((lat, width), F32),
            vm((lat, width), BF16),
            vm((lat, width), BF16),
            vm(packed, BF16),
            vm((Z,) + packed, BF16),
            vm((Z, pad, width), BF16),
            vm((Z, rows, lat), F32),
            vm((B, n, rows, lat), F32),
            vm((8, lat), F32),
            vm((n, 8, lat), F32),
            vm((1, lat), F32),
            vm((Z, pad, lat), BF16),
            vm((rows, width), F32),
            vm((Z,) + packed, BF16),
            vm((Z,) + packed, BF16),
            vm(packed, BF16),
            vm((Z,) + packed, BF16),
            vm((Z, pad, width), BF16),
            vm((Z, rows, lat), F32),
            vm((B, n, rows, lat), F32),
            vm((Z, pad, lat), BF16),
            vm((1, width), F32),
            vm((1, min(256, width)), F32),
            vm((Z, 8, 128), F32),
            vm((8, 128), F32),
            vm((n, 8, 128), F32),
            dma((2,)),
            dma((Z,)),
            dma((Z,)),
            dma((Z,)),
            dma((B, n)),
            dma((n,)),
            dma((n,)),
            dma((B, n)),
            dma((Z,)),
            dma((Z,)),
            dma((Z,)),
            dma((Z,)),
            dma((Z,)),
            dma((Z,)),
            dma((B, n)),
            dma((B, n)),
            dma((Z,)),
            dma((Z,)),
            dma((Z,)),
            dma((n,)),
            dma((n,)),
        ],
        compiler_params=pltpu.CompilerParams(
            collective_id=0, has_side_effects=True, vmem_limit_bytes=36 * 1024 * 1024
        ),
    )(inputs, dec_bias.reshape(1, -1), enc_bias.reshape(1, -1), enc_master, dec_master)


def per_device(
    Z, X, C,
    inputs, dec_bias, enc_master, enc_bias, dec_master, enc_m, enc_v, dec_m, dec_v, bias_m, bias_v,
):
    enc_grad, dec_grad, bias_grad, scalars = gradients(
        Z, X, C, inputs, dec_bias, enc_bias, enc_master, dec_master
    )
    clip_scale = scalars[0, 1]
    bias_grad = bias_grad.reshape(-1)
    enc_new, enc_m_new, enc_v_new = adam_update(enc_master, enc_m, enc_v, clip_scale * enc_grad)
    bias_new, bias_m_new, bias_v_new = adam_update(enc_bias, bias_m, bias_v, clip_scale * bias_grad)
    dec_new, dec_m_new, dec_v_new = adam_update(dec_master, dec_m, dec_v, clip_scale * dec_grad)
    return (
        enc_new,
        bias_new,
        dec_new,
        enc_m_new,
        enc_v_new,
        dec_m_new,
        dec_v_new,
        bias_m_new,
        bias_v_new,
        scalars[0, :1],
    )


def solution(mesh):
    matrix = P(("groups", "latent"), ("dp", "sub"))
    vector = P(("groups", "latent"))
    sizes = (mesh.shape["latent"], mesh.shape["dp"], mesh.shape["sub"])
    return jax.shard_map(
        functools.partial(per_device, *sizes),
        mesh=mesh,
        in_specs=(
            matrix, P(("groups", "dp", "sub")), matrix, vector, matrix,
            matrix, matrix, matrix, matrix, vector, vector,
        ),
        out_specs=(
            matrix, vector, matrix, matrix, matrix, matrix, matrix, vector, vector, P("groups"),
        ),
        check_vma=False,
    )
```

time: 193 us -> 71.4 us (0.37)
  waiting for transfers between devices: 82.8 us -> 0 us
  blocking collectives: 70.8 us -> 0 us
  Pallas kernels: 0 us -> 58.1 us
  between operations: 19.5 us -> 0.69 us
  matrix products: 8.34 us -> 0 us
  local copies, waits for them, and re-layouts: 0.7 us -> 5.83 us
  other arithmetic: 10.4 us -> 6.4 us
    psum x2 -> x0, waiting for transfers between devices: 62.6 us -> none  [the longest x1 33 us: per_device(): pre_total, norm_total = lax.psum((pre_part, norm_part), ('dp', 'sub'))]
    pallas_call x0 -> x1, Pallas kernels: none -> 58.1 us  [gradients(): pl.pallas_call(functools.partial(kernel, Z, X, C, rows), out_shape=(big,...]
    psum x2 -> x0, blocking collectives: 38.4 us -> none  [the longest x1 32.7 us: per_device(): grad_square = lax.psum(square_part, ('latent', 'dp', 'sub'))]
    all_gather x2 -> x0, blocking collectives: 32.4 us -> none  [the longest x1 17 us: per_device(): gathered = lax.all_gather(inputs, 'latent', axis=0, tiled=True)]
    reduce_scatter x1 -> x0, waiting for transfers between devices: 20.1 us -> none  [per_device(): lax.psum_scatter(partial_value, 'latent', scatter_dimension=0, tiled=True)]
    dot_general x5 -> x0, matrix products: 8.34 us -> none  [the longest x1 2.24 us: per_device(): lax.dot_general(centered, enc_copy, contract, preferred_element_type=jnp....]
    unnamed x22 -> x18, local copies, waits for them, and re-layouts: 0.7 us -> 5.24 us
    reduce_sum x4 -> x0, other arithmetic: 4.21 us -> none  [the longest x1 1.87 us: per_device(): sparse_part = own_flag * jnp.sum(active * dec_norms)]
  transfers between devices with their start and end apart: 3 -> 0, of which waited for: 3 -> 0; matrix products, arithmetic and copies ran while one was open for 0% -> 0% of each run, Pallas kernels for 0% -> 0%
where the time goes in v1:
time: 71.4 us; the launch traced here: 71.1 us
  Pallas kernels  58.1 us (81%)
  other arithmetic  6.4 us (9%)
  local copies, waits for them, and re-layouts  5.83 us (8%)
    pallas_call x1, Pallas kernels, gradients(): pl.pallas_call(functools.partial(kernel, Z, X, C, rows), out_shape=(big,...  58.1 us
    sub x2, other arithmetic, adam_update(): master - learn_rate * (new_one / fix_one) / (jnp.sqrt(new_two / fix_two)...  5.76 us
    unnamed x18, local copies, waits for them, and re-layouts  5.24 us

profile of v1, /device:TPU:0, one launch (start us, length us, event | category | flops | bytes accessed | tf_op | source)
XLA Modules:
  0.0 71.1 jit_solution(17700413233335532373)
XLA Ops:
  0.6 0.0 copy-start.4
  0.7 0.7 copy-done.4
  1.3 0.0 copy-start
  1.3 1.2 %copy-done = f32[208,1024]{1,0:T(8,128)S(1)} copy-done((f32[208,1024]{1,0:T(8,128)S(1)}, f32[208,1024]{1,0:T(8,128)}, u32[]{:S(2)}) %copy-start) | copy-done | bytes 851992
  2.5 0.0 copy-start.1
  2.5 1.2 %copy-done.1 = f32[208,1024]{1,0:T(8,128)S(1)} copy-done((f32[208,1024]{1,0:T(8,128)S(1)}, f32[208,1024]{1,0:T(8,128)}, u32[]{:S(2)}) %copy-start.1) | copy-done | bytes 851992
  3.6 0.0 copy-start.2
  3.6 0.9 %copy-done.2 = bf16[56,1024]{1,0:T(8,128)(2,1)S(1)} copy-done((bf16[56,1024]{1,0:T(8,128)(2,1)S(1)}, bf16[56,1024]{1,0:T(8,128)(2,1)}, u32[]{:S(2)}) %copy-start.2) | copy-done | bytes 114712
  4.5 0.0 copy-start.3
  4.5 0.7 copy-done.3
  5.2 0.0 copy-start.5
  5.2 0.0 copy-start.6
  5.2 58.1 %shard_map.186 = (f32[208,1024]{1,0:T(8,128)S(1)}, f32[208,1024]{1,0:T(8,128)S(1)}, f32[1,208]{1,0:T(1,128)S(1)}, f32[8,128]{1,0:T(8,128)S(1)}) custom-call(bf16[56,1024]{1,0:T(8,128)(2,1)S(1)} %copy-done.2, f32[1,1024]{1,0:T(1,128)S(1)} %bitcast.5, f32[1,208]{1,0:T(1,128)S(1)} %bitcast.6, f32[208,1024]{1,0:T(8,128)S(1)} %copy-done.1, f32[208,1024]{1,0:T(8,128)S(1)} %copy-done), custom_call_target="tpu_custom_call" | custom-call | tf_op jit(solution)/shard_map/pallas_call | solution.py:399
  63.4 0.6 fusion.6
  64.0 0.0 copy-done.5
  64.0 0.0 copy-done.6
  64.0 0.0 copy-start.8
  64.0 5.2 %divide_subtract_fusion = (f32[208,1024]{1,0:T(8,128)}, f32[208,1024]{1,0:T(8,128)}, f32[208,1024]{1,0:T(8,128)}, f32[208,1024]{1,0:T(8,128)}, f32[208,1024]{1,0:T(8,128)}, /*index=5*/f32[208,1024]{1,0:T(8,128)}) fusion(f32[208,1024]{1,0:T(8,128)S(1)} %copy-done, f32[208,1024]{1,0:T(8,128)S(1)} %get-tuple-element.17, f32[]{:T(128)} %bitcast.2, ...), kind=kLoop, calls=%fused_computation.4 | loop fusion | flops 5537792 | bytes 11927556 | tf_op jit(solution)/shard_map/sub | solution.py:29
  69.1 0.6 broadcast_multiply_fusion
  69.8 0.0 copy-start.7
  69.8 0.0 copy-done.8
  69.8 0.7 copy-done.7
  70.5 0.6 divide_subtract_fusion.2
Async XLA Ops:
  0.6 0.7 copy-start.4
  1.3 1.2 %copy-start = (f32[208,1024]{1,0:T(8,128)S(1)}, f32[208,1024]{1,0:T(8,128)}, u32[]{:S(2)}) copy-start(f32[208,1024]{1,0:T(8,128)} %dec_hbm.1) | copy-start | bytes 2555908
  2.5 1.2 %copy-start.1 = (f32[208,1024]{1,0:T(8,128)S(1)}, f32[208,1024]{1,0:T(8,128)}, u32[]{:S(2)}) copy-start(f32[208,1024]{1,0:T(8,128)} %enc_hbm.1) | copy-start | bytes 2555908
  3.6 0.9 %copy-start.2 = (bf16[56,1024]{1,0:T(8,128)(2,1)S(1)}, bf16[56,1024]{1,0:T(8,128)(2,1)}, u32[]{:S(2)}) copy-start(bf16[56,1024]{1,0:T(8,128)(2,1)} %x_ref.1) | copy-start | bytes 344068
  4.5 0.7 copy-start.3
  5.2 58.7 %copy-start.5 = (f32[208,1024]{1,0:T(8,128)S(1)}, f32[208,1024]{1,0:T(8,128)}, u32[]{:S(2)}) copy-start(f32[208,1024]{1,0:T(8,128)} %param.18) | copy-start | bytes 2555908
  5.2 58.7 %copy-start.6 = (f32[208,1024]{1,0:T(8,128)S(1)}, f32[208,1024]{1,0:T(8,128)}, u32[]{:S(2)}) copy-start(f32[208,1024]{1,0:T(8,128)} %param.19) | copy-start | bytes 2555908
  64.0 5.8 %copy-start.8 = (f32[208]{0:T(256)S(1)}, f32[208]{0:T(256)}, u32[]{:S(2)}) copy-start(f32[208]{0:T(256)} %param.21) | copy-start | bytes 2500
  69.8 0.7 copy-start.7

commit v2 on v1

--- a/solution.py
+++ b/solution.py
@@ -45,9 +45,9 @@
 
 
 def kernel(
-    Z, X, C, rows, x_ref, bias_ref, enc_bias_ref, enc_hbm, dec_hbm,
+    Z, X, C, rows, x_hbm, bias_hbm, enc_bias_hbm, enc_hbm, dec_hbm,
     enc_grad_ref, dec_grad_ref, bias_grad_ref, scalar_ref,
-    enc_f, dec_f, enc_b, dec_b,
+    x_ref, bias_ref, enc_bias_ref, enc_f, dec_f, enc_b, dec_b,
     cent_tx, cent_rx, cent, part_tx, part_rx, norm_tx, norm_rx, norm_row, act, recon_own,
     recon_tx, recon_rx, grad_tx, grad_rx, grad, back_tx, back_rx, pre, loss_acc, square_acc,
     one_rx, two_tx, two_rx,
@@ -79,10 +79,13 @@
             src_ref=src, dst_ref=dst, send_sem=s, recv_sem=r, device_id=dev, device_id_type=MESH
         )
 
-    load_enc = pltpu.make_async_copy(enc_hbm, enc_f, load_sem.at[0])
-    load_dec = pltpu.make_async_copy(dec_hbm, dec_f, load_sem.at[1])
-    load_enc.start()
-    load_dec.start()
+    load_x = pltpu.make_async_copy(x_hbm, x_ref, load_sem.at[0])
+    load_bias = pltpu.make_async_copy(bias_hbm, bias_ref, load_sem.at[1])
+    load_dec = pltpu.make_async_copy(dec_hbm, dec_f, load_sem.at[2])
+    load_enc = pltpu.make_async_copy(enc_hbm, enc_f, load_sem.at[3])
+    load_enc_bias = pltpu.make_async_copy(enc_bias_hbm, enc_bias_ref, load_sem.at[4])
+    for load in (load_x, load_bias, load_dec, load_enc, load_enc_bias):
+        load.start()
 
     barrier = pltpu.get_barrier_semaphore()
     for k in range(1, Z):
@@ -102,20 +105,54 @@
         ref[:rows, half:] = right.astype(BF16)
         ref[rows:, :] = jnp.zeros((pad - rows, width), BF16)
 
+    load_x.wait()
+    load_bias.wait()
     x_own = x_ref[...].astype(F32)
     centered = x_own - bias_ref[...]
     pack(cent_tx, centered)
     place(cent.at[0], centered[:, :half], centered[:, half:])
     pl.semaphore_wait(barrier, Z - 1 + n - 1)
 
-    def cent_copy(k):
-        return remote(cent_tx, cent_rx.at[Z - k], cent_s.at[k], cent_r.at[Z - k], zdev(k))
+    fewer = jnp.minimum(z, Z - 1 - z)
+
+    def nearest(t):
+        paired = t <= 2 * fewer
+        distance = jnp.where(paired, (t + 1) // 2, t - fewer)
+        low = jnp.where(paired, t % 2, jnp.where(z > Z - 1 - z, 1, 0)) == 1
+        return jnp.where(low, Z - distance, distance), low
+
+    def neighbour_copies(tx, rx, s, r, action):
+        @pl.when(z < Z - 1)
+        def _():
+            action(remote(tx, rx.at[Z - 1], s.at[0], r.at[Z - 1], {"latent": z + 1}))
+
+        @pl.when(z > 0)
+        def _():
+            action(remote(tx, rx.at[1], s.at[Z], r.at[1], {"latent": z - 1}))
+
+    def onward(rx, s, r, t, action):
+        j, low = nearest(t)
+        step = jnp.where(low, 1, -1)
+        target = z + step
+
+        @pl.when(jnp.logical_and(target >= 0, target < Z))
+        def _():
+            action(remote(rx.at[j], rx.at[j - step], s.at[j], r.at[j - step], {"latent": target}))
+
+    def relay(rx, s, r, t):
+        j, _ = nearest(t)
+        remote(rx.at[j], rx.at[j], s.at[0], r.at[j], zdev(1)).wait_recv()
+        onward(rx, s, r, t, start)
+        return j
+
+    def start(copy):
+        copy.start()
+
+    def wait_send(copy):
+        copy.wait_send()
 
     def recon_copy(j):
         return remote(recon_tx.at[j], recon_rx.at[Z - j], recon_s.at[j], recon_r.at[Z - j], zdev(j))
-
-    def grad_copy(k):
-        return remote(grad_tx, grad_rx.at[Z - k], grad_s.at[k], grad_r.at[Z - k], zdev(k))
 
     def norm_copy(k):
         return remote(norm_tx, norm_rx.at[f], norm_s.at[k], norm_r.at[f], fdev(fpeer(k)))
@@ -133,8 +170,7 @@
     def shared(buf, s, r, j):
         return remote(buf.at[j], buf.at[j], s.at[0, 0], r.at[j], fdev(fpeer(1)))
 
-    for k in range(1, Z):
-        cent_copy(k).start()
+    neighbour_copies(cent_tx, cent_rx, cent_s, cent_r, start)
 
     load_dec.wait()
     dec = dec_f[...]
@@ -149,6 +185,7 @@
     for k in range(1, n):
         norm_copy(k).start()
     load_enc.wait()
+    load_enc_bias.wait()
     enc_b[...] = enc_f[...].astype(BF16)
     loss_acc[...] = jnp.zeros_like(loss_acc)
 
@@ -178,16 +215,23 @@
         for k in range(1, n):
             share_copy(buf, s, r, j, k).start()
 
-    def encode(j):
-        @when(j > 0)
-        def _():
-            remote(cent_tx, cent_rx.at[j], cent_s.at[0], cent_r.at[j], zdev(1)).wait_recv()
+    def block_of(t):
+        return 0 if isinstance(t, int) and t == 0 else nearest(t)[0]
+
+    def encode(t):
+        j = block_of(t)
+
+        @when(t > 0)
+        def _():
+            relay(cent_rx, cent_s, cent_r, t)
             place(cent.at[j], *unpack(cent_rx.at[j]))
 
         value = lax.dot_general(cent[j], enc_b[...], NT, preferred_element_type=F32)[:rows]
         send_part(value, part_tx, part_rx, part_s, part_r, j)
 
-    def activate(j):
+    def activate(t):
+        j = block_of(t)
+
         @pl.when(f == j // B)
         def _():
             total = sum_parts(part_rx, part_s, part_r, j % B)
@@ -197,18 +241,20 @@
                 active * norm_row[...], axis=0, keepdims=True
             )
 
-    def decode(j):
+    def decode(t):
+        j = block_of(t)
+
         @pl.when(f != j // B)
         def _():
             shared(act, act_s, act_r, j).wait_recv()
 
         value = jnp.dot(act[j], dec_b[...], preferred_element_type=F32)[:rows]
 
-        @when(j == 0)
+        @when(t == 0)
         def _():
             recon_own[...] = value
 
-        @when(j > 0)
+        @when(t > 0)
         def _():
             pack(recon_tx.at[j], value)
             recon_copy(j).start()
@@ -235,9 +281,9 @@
             decode(s - 2)
     else:
         finish_norms()
-        steps(0, Z, encode, False)
-        steps(0, Z, activate, False)
-        steps(0, Z, decode, False)
+        for stage in (encode, activate, decode):
+            stage(0)
+            steps(1, Z, stage, False)
 
     left = recon_own[:, :half]
     right = recon_own[:, half:]
@@ -255,22 +301,25 @@
     residual = jnp.concatenate([left, right], axis=1) + bias_ref[...] - x_own
     out_grad = residual * (2.0 / tokens)
     pack(grad_tx, out_grad)
-    for k in range(1, Z):
-        grad_copy(k).start()
+    neighbour_copies(grad_tx, grad_rx, grad_s, grad_r, start)
     place(grad.at[0], out_grad[:, :half], out_grad[:, half:])
     error = jnp.sum(residual * residual, axis=0, keepdims=True)
     loss_acc[...] += error
 
-    def back(j):
-        @when(j > 0)
-        def _():
-            remote(grad_tx, grad_rx.at[j], grad_s.at[0], grad_r.at[j], zdev(1)).wait_recv()
+    def back(t):
+        j = block_of(t)
+
+        @when(t > 0)
+        def _():
+            relay(grad_rx, grad_s, grad_r, t)
             place(grad.at[j], *unpack(grad_rx.at[j]))
 
         value = lax.dot_general(grad[j], dec_b[...], NT, preferred_element_type=F32)[:rows]
         send_part(value, back_tx, back_rx, back_s, back_r, j)
 
-    def through(j):
+    def through(t):
+        j = block_of(t)
+
         @pl.when(f == j // B)
         def _():
             total = sum_parts(back_rx, back_s, back_r, j % B)
@@ -285,8 +334,9 @@
                 back(s)
             through(s - 1)
     else:
-        steps(0, Z, back, False)
-        steps(0, Z, through, False)
+        for stage in (back, through):
+            stage(0)
+            steps(1, Z, stage, False)
 
     act_all = act[...].reshape(Z * pad, lat)
     act_sum = jnp.sum(act_all.astype(F32), axis=0, keepdims=True)
@@ -358,17 +408,20 @@
     scalar_ref[...] = jnp.where(lane == 0, total * (1.0 / tokens), scale)
 
     for k in range(1, Z):
-        cent_copy(k).wait_send()
-        grad_copy(k).wait_send()
         one_copy(k).wait_send()
     for k in range(1, n):
         norm_copy(k).wait_send()
         two_copy(k).wait_send()
 
+    neighbour_copies(cent_tx, cent_rx, cent_s, cent_r, wait_send)
+    neighbour_copies(grad_tx, grad_rx, grad_s, grad_r, wait_send)
+
     def drain(j):
         @when(j > 0)
         def _():
             recon_copy(j).wait_send()
+            onward(cent_rx, cent_s, cent_r, j, wait_send)
+            onward(grad_rx, grad_s, grad_r, j, wait_send)
 
         @pl.when(f != j // B)
         def _():
@@ -394,7 +447,7 @@
     vm = pltpu.VMEM
     big = jax.ShapeDtypeStruct((lat, width), F32)
     vmem = pl.BlockSpec(memory_space=pltpu.VMEM)
-    hbm = pl.BlockSpec(memory_space=pl.ANY)
+    hbm = pl.BlockSpec(memory_space=pltpu.HBM)
     packed = (2 * rows, width // 2)
     return pl.pallas_call(
         functools.partial(kernel, Z, X, C, rows),
@@ -404,9 +457,12 @@
             jax.ShapeDtypeStruct((1, lat), F32),
             jax.ShapeDtypeStruct((8, 128), F32),
         ),
-        in_specs=[vmem, vmem, vmem, hbm, hbm],
+        in_specs=[hbm] * 5,
         out_specs=[vmem] * 4,
         scratch_shapes=[
+            vm((rows, width), BF16),
+            vm((1, width), F32),
+            vm((1, lat), F32),
             vm((lat, width), F32),
             vm((lat, width), F32),
             vm((lat, width), BF16),
@@ -434,8 +490,8 @@
             vm((Z, 8, 128), F32),
             vm((8, 128), F32),
             vm((n, 8, 128), F32),
-            dma((2,)),
-            dma((Z,)),
+            dma((5,)),
+            dma((Z + 1,)),
             dma((Z,)),
             dma((Z,)),
             dma((B, n)),
@@ -445,7 +501,7 @@
             dma((Z,)),
             dma((Z,)),
             dma((Z,)),
-            dma((Z,)),
+            dma((Z + 1,)),
             dma((Z,)),
             dma((Z,)),
             dma((B, n)),
@@ -457,7 +513,7 @@
             dma((n,)),
         ],
         compiler_params=pltpu.CompilerParams(
-            collective_id=0, has_side_effects=True, vmem_limit_bytes=36 * 1024 * 1024
+            collective_id=0, has_side_effects=True, vmem_limit_bytes=60 * 1024 * 1024
         ),
     )(inputs, dec_bias.reshape(1, -1), enc_bias.reshape(1, -1), enc_master, dec_master)
 

time: 71.4 us -> 65.6 us (0.919)
  Pallas kernels: 58.1 us -> 54.5 us
  local copies, waits for them, and re-layouts: 5.83 us -> 2.67 us
  other arithmetic: 6.4 us -> 7.54 us
    unnamed x18 -> x12, local copies, waits for them, and re-layouts: 5.24 us -> 1.33 us
    pallas_call x1, Pallas kernels: 58.1 us -> 54.5 us  [gradients(): pl.pallas_call(functools.partial(kernel, Z, X, C, rows), out_shape=(big,...]
    sub x2, other arithmetic: 5.76 us -> 6.9 us  [adam_update(): master - learn_rate * (new_one / fix_one) / (jnp.sqrt(new_two / fix_two)...]
    slice x1, local copies, waits for them, and re-layouts: 0.58 us -> 1.34 us  [per_device(): scalars[0, :1]]
where the time goes in v2:
time: 65.6 us; the launch traced here: 65.4 us
  Pallas kernels  54.5 us (83%)
  other arithmetic  7.54 us (11%)
  local copies, waits for them, and re-layouts  2.67 us (4%)
  between operations  0.71 us (1%)
    pallas_call x1, Pallas kernels, gradients(): pl.pallas_call(functools.partial(kernel, Z, X, C, rows), out_shape=(big,...  54.5 us
    sub x2, other arithmetic, adam_update(): master - learn_rate * (new_one / fix_one) / (jnp.sqrt(new_two / fix_two)...  6.9 us
    slice x1, local copies, waits for them, and re-layouts, per_device(): scalars[0, :1]  1.34 us
    unnamed x12, local copies, waits for them, and re-layouts  1.33 us

profile of v2, /device:TPU:0, one launch (start us, length us, event | category | flops | bytes accessed | tf_op | source)
XLA Modules:
  0.0 65.4 jit_solution(14483585105961993543)
XLA Ops:
  0.6 0.0 copy-start
  0.7 0.0 copy-start.1
  0.7 54.5 %shard_map.186 = (f32[208,1024]{1,0:T(8,128)}, f32[208,1024]{1,0:T(8,128)}, f32[1,208]{1,0:T(1,128)}, f32[8,128]{1,0:T(8,128)}) custom-call(bf16[56,1024]{1,0:T(8,128)(2,1)} %x_hbm.1, f32[1,1024]{1,0:T(1,128)} %bitcast.5, f32[1,208]{1,0:T(1,128)} %bitcast.6, f32[208,1024]{1,0:T(8,128)} %enc_hbm.1, f32[208,1024]{1,0:T(8,128)} %dec_hbm.1), custom_call_target="tpu_custom_call" | custom-call | tf_op jit(solution)/shard_map/pallas_call | solution.py:452
  55.1 1.3 %fusion.6 = (f32[1,1]{1,0:T(1,128)}, f32[1,1]{1,0:T(1,128)}) fusion(f32[8,128]{1,0:T(8,128)} %get-tuple-element.14), kind=kLoop, calls=%fused_computation.13 | loop fusion | bytes 16 | tf_op jit(solution)/shard_map/slice | solution.py:543
  56.5 0.0 copy-done
  56.5 0.0 copy-done.1
  56.5 0.0 copy-start.3
  56.5 0.0 copy-start.4
  56.5 6.3 %divide_subtract_fusion = (f32[208,1024]{1,0:T(8,128)}, f32[208,1024]{1,0:T(8,128)}, f32[208,1024]{1,0:T(8,128)}, f32[208,1024]{1,0:T(8,128)}, f32[208,1024]{1,0:T(8,128)}, /*index=5*/f32[208,1024]{1,0:T(8,128)}) fusion(f32[208,1024]{1,0:T(8,128)S(1)} %copy-done, f32[208,1024]{1,0:T(8,128)} %get-tuple-element.17, f32[]{:T(128)} %bitcast.2, ...), kind=kLoop, calls=%fused_computation.4 | loop fusion | flops 5537792 | bytes 11927556 | tf_op jit(solution)/shard_map/sub | solution.py:29
  62.8 0.0 copy-start.5
  62.8 0.7 %copy-done.5 = f32[1,208]{1,0:T(1,128)S(1)} copy-done((f32[1,208]{1,0:T(1,128)S(1)}, f32[1,208]{1,0:T(1,128)}, u32[]{:S(2)}) %copy-start.5) | copy-done | bytes 856
  63.5 0.6 broadcast_multiply_fusion
  64.1 0.0 copy-start.2
  64.1 0.0 copy-done.3
  64.1 0.0 copy-done.4
  64.2 0.7 copy-done.2
  64.8 0.6 divide_subtract_fusion.2
Async XLA Ops:
  0.6 55.8 %copy-start = (f32[208,1024]{1,0:T(8,128)S(1)}, f32[208,1024]{1,0:T(8,128)}, u32[]{:S(2)}) copy-start(f32[208,1024]{1,0:T(8,128)} %dec_hbm.1) | copy-start | bytes 2555908
  0.7 55.8 %copy-start.1 = (f32[208,1024]{1,0:T(8,128)S(1)}, f32[208,1024]{1,0:T(8,128)}, u32[]{:S(2)}) copy-start(f32[208,1024]{1,0:T(8,128)} %enc_hbm.1) | copy-start | bytes 2555908
  56.5 7.7 %copy-start.3 = (f32[208]{0:T(256)S(1)}, f32[208]{0:T(256)}, u32[]{:S(2)}) copy-start(f32[208]{0:T(256)} %param.20) | copy-start | bytes 2500
  56.5 7.7 %copy-start.4 = (f32[208]{0:T(256)S(1)}, f32[208]{0:T(256)}, u32[]{:S(2)}) copy-start(f32[208]{0:T(256)} %param.21) | copy-start | bytes 2500
  62.8 0.7 %copy-start.5 = (f32[1,208]{1,0:T(1,128)S(1)}, f32[1,208]{1,0:T(1,128)}, u32[]{:S(2)}) copy-start(f32[1,208]{1,0:T(1,128)} %get-tuple-element.16) | copy-start | bytes 2500
  64.1 0.7 %copy-start.2 = (f32[208]{0:T(256)S(1)}, f32[208]{0:T(256)}, u32[]{:S(2)}) copy-start(f32[208]{0:T(256)} %param.14) | copy-start | bytes 2500
